TPU v7x, 512 devices: a whole 4x4x16 slice. The times are simulated.
512 devices in a mesh: ctx: 32 (over z_lo, y), grp: 16 (over x, z_hi, core).
Axes of the slice: x: 4, y: 4, z: 16 (z_hi: 2, z_lo: 8; z = z_hi * 8 + z_lo), core: 2. Of those that a mesh axis runs over, the one named last changes fastest.
Arguments:
- q_nope: bfloat16 [256, 128, 128], P(None, 'ctx'), may hold values from -6 to 6
- q_rope: bfloat16 [256, 128, 64], P(None, 'ctx'), may hold values from -720 to 720
- w_uk: bfloat16 [128, 128, 512], P('ctx'), may hold values from -0.5 to 0.5
- w_uv: bfloat16 [128, 512, 128], P('ctx'), may hold values from -0.375 to 0.375
- prompt: bfloat16 [6144, 576], P('grp'), may hold values from -12 to 12
- w_out: bfloat16 [16384, 7168], P('ctx', 'grp'), may hold values from -0.0625 to 0.0625
- residual: bfloat16 [256, 7168], P('ctx', 'grp'), may hold values from -3 to 3
- routes: int32 [256, 8], P('ctx'), may hold values from 0 to 31, all different within a row; in each aligned block of 8 rows (0 to 7, 8 to 15, ...) at most 4 rows name the same one
- route_scores: float32 [256, 8], P('ctx'), may hold values from 0.05 to 1
- expert_gate: bfloat16 [32, 7168, 1024], P('ctx', 'grp'), may hold values from -0.0625 to 0.0625
- expert_up: bfloat16 [32, 7168, 1024], P('ctx', 'grp'), may hold values from -0.0625 to 0.0625
- expert_down: bfloat16 [32, 1024, 7168], P('ctx', None, 'grp'), may hold values from -0.1875 to 0.1875
Outputs:
- layer_out: bfloat16 [256, 7168], P('ctx', 'grp')
Inputs may be any that keep to these rules, and one draw needn't show every extreme that they name: `routes`: in each aligned block of 8 rows no expert is named by more than 4 rows, a bound that some block reaches; the 8 experts of a row differ.
All inputs are finite; a program needn't handle non-finite values.
Results may differ from a plain program's by a relative error of at most 0.0163.
Values may be sent and summed in bfloat16 or wider, within the bound.
A program may use at most 64 MiB of HBM per device.

v0:
```python
import jax
import jax.numpy as jnp
from jax import lax
from jax.sharding import PartitionSpec as P

NOPE = 128
ROPE = 64
LAT = 512
VDIM = 128
CAP = 4
route_factor = 2.5


def per_device(
    q_nope,
    q_rope,
    w_uk,
    w_uv,
    prompt,
    w_out,
    residual,
    routes,
    route_scores,
    expert_gate,
    expert_up,
    expert_down,
):
    score_scale = (NOPE + ROPE) ** (-0.5)
    q_latent = jnp.einsum("rhn,hnl->rhl", q_nope, w_uk, preferred_element_type=jnp.float32).astype(
        jnp.bfloat16
    )
    queries = jnp.concatenate([q_latent, q_rope], axis=-1)
    head_uv = w_uv.astype(jnp.float32)
    head_cols = queries.shape[1] * VDIM
    all_keys = lax.all_gather(prompt, "grp", axis=0, tiled=True)
    row_share = queries.shape[0] // lax.axis_size("grp")
    own_queries = lax.dynamic_slice_in_dim(queries, lax.axis_index("grp") * row_share, row_share, 0)
    scores = (
        jnp.einsum("rhc,jc->rhj", own_queries, all_keys, preferred_element_type=jnp.float32)
        * score_scale
    )
    top_score = jnp.max(scores, axis=-1)
    raised = jnp.exp(scores - top_score[..., None])
    denominator = jnp.sum(raised, axis=-1)
    weighted = jnp.einsum(
        "rhj,jl->rhl",
        raised.astype(jnp.bfloat16),
        all_keys[:, :LAT],
        preferred_element_type=jnp.float32,
    )
    values = jnp.einsum("rhl,hlv->rhv", weighted, head_uv, precision=lax.Precision.HIGHEST)
    top_score, denominator, values = (top_score, denominator, values)
    own_rows = (values / denominator[..., None]).astype(jnp.bfloat16).reshape(row_share, head_cols)
    attended = lax.all_gather(own_rows, "grp", axis=0, tiled=True)
    local_rows = residual.shape[0]
    projected = lax.psum_scatter(
        jnp.dot(attended, w_out, preferred_element_type=jnp.float32),
        "ctx",
        scatter_dimension=0,
        tiled=True,
    )
    hidden = residual.astype(jnp.float32) + projected
    moe_input = hidden.astype(jnp.bfloat16)
    gate_weights = route_factor * route_scores / jnp.sum(route_scores, axis=-1, keepdims=True)
    top_count = routes.shape[1]
    experts = expert_gate.shape[0] * lax.axis_size("ctx")
    flat_routes = routes.reshape(-1)
    onehot = (flat_routes[:, None] == jnp.arange(experts, dtype=jnp.int32)[None, :]).astype(
        jnp.int32
    )
    before = jnp.cumsum(onehot, axis=0) - onehot
    slot_index = jnp.sum(before * onehot, axis=1)
    target = flat_routes * CAP + slot_index
    select = (target[:, None] == jnp.arange(experts * CAP, dtype=jnp.int32)[None, :]).astype(
        jnp.float32
    )
    row_of = jnp.arange(local_rows * top_count, dtype=jnp.int32) // top_count
    row_pick = (row_of[:, None] == jnp.arange(local_rows, dtype=jnp.int32)[None, :]).astype(
        jnp.float32
    )
    slot_rows = jnp.dot(select.T, row_pick, precision=lax.Precision.HIGHEST)
    outgoing = jnp.dot(
        slot_rows.astype(jnp.bfloat16), moe_input, preferred_element_type=jnp.float32
    ).astype(jnp.bfloat16)
    outgoing = outgoing.reshape(experts, 1, CAP, moe_input.shape[1])
    slot_weights = jnp.dot(
        row_pick.T, select * gate_weights.reshape(-1)[:, None], precision=lax.Precision.HIGHEST
    )
    arrived = lax.all_to_all(outgoing, "ctx", split_axis=0, concat_axis=1, tiled=True)
    gate_part = jnp.einsum(
        "escd,edf->escf", arrived, expert_gate, preferred_element_type=jnp.float32
    )
    up_part = jnp.einsum("escd,edf->escf", arrived, expert_up, preferred_element_type=jnp.float32)
    gate_sum, up_sum = lax.psum((gate_part, up_part), "grp")
    activated = (jax.nn.silu(gate_sum) * up_sum).astype(jnp.bfloat16)
    result = jnp.einsum(
        "escf,efd->escd", activated, expert_down, preferred_element_type=jnp.float32
    ).astype(jnp.bfloat16)
    returned = lax.all_to_all(result, "ctx", split_axis=1, concat_axis=0, tiled=True)
    returned = returned.reshape(experts * CAP, moe_input.shape[1]).astype(jnp.float32)
    combined = jnp.dot(slot_weights, returned, precision=lax.Precision.HIGHEST)
    return (hidden + combined).astype(jnp.bfloat16)


def solution(mesh):
    in_specs = (
        P(None, "ctx", None),
        P(None, "ctx", None),
        P("ctx", None, None),
        P("ctx", None, None),
        P("grp", None),
        P("ctx", "grp"),
        P("ctx", "grp"),
        P("ctx", None),
        P("ctx", None),
        P("ctx", "grp", None),
        P("ctx", "grp", None),
        P("ctx", None, "grp"),
    )
    out_specs = P("ctx", "grp")
    return jax.shard_map(
        per_device, mesh=mesh, in_specs=in_specs, out_specs=out_specs, check_vma=False
    )
```

profile of v0, /device:TPU:8, one launch (start us, length us, event | category | flops | bytes accessed | tf_op | source)
XLA Modules:
  0.0 793.5 jit_solution(4318295882476667328)
XLA Ops:
  6.5 0.0 copy-start
  6.5 0.0 all-gather.2.cloned.1.call-start
  6.5 0.7 all-gather.2.cloned.1.call-update
  7.3 0.0 reduce-scatter.2.cloned.1.call-start
  7.3 1.6 fusion.8
  8.9 171.5 %all-gather.2.cloned.1.call-done = bf16[6144,576]{0,1:T(8,128)(2,1)} async-done(((bf16[384,576]{0,1:T(8,128)(2,1)}), bf16[6144,576]{0,1:T(8,128)(2,1)}) %all-gather.2.cloned.1.call-update) | async-done | bytes 7077904 | tf_op jit(solution)/shard_map/all_gather | solution.py:35
  180.4 0.0 copy-done.5
  180.4 4.4 fusion.42
  184.8 0.4 fusion.6
  185.2 0.3 copy-done.1
  185.5 2.0 fusion.5
  187.6 0.0 copy-done.3
  187.6 0.0 copy-start.9
  187.6 0.0 copy-start.7
  187.6 0.3 fusion.12
  187.9 35.3 %all_gather.7 = bf16[256,512]{1,0:T(8,128)(2,1)S(1)} all-gather(bf16[16,512]{1,0:T(8,128)(2,1)S(1)} %bitcast.63), channel_id=1, replica_groups=mesh['ctx'=32,'grp'=16] {'grp'}, dimensions={0}, use_global_device_ids=true | all-gather | bytes 278528 | tf_op jit(solution)/shard_map/all_gather | solution.py:54
  223.3 0.0 copy-done.4
  223.3 1.1 fusion.43
  224.4 0.0 reduce-scatter.2.cloned.1.call-update
  224.4 0.0 all-reduce.3.cloned.1.call-start
  224.4 0.0 copy-done.9
  224.5 0.1 reshape.68
  224.5 0.1 fusion.29
  224.6 0.1 reduce_window_sum.11
  224.7 0.2 select_reduce_fusion
  224.9 0.3 convolution_convert_fusion.3
  225.2 228.0 %reduce-scatter.2.cloned.1.call-done = f32[8,448]{1,0:T(8,128)} async-done(((f32[256,448]{1,0:T(8,128)}), f32[8,448]{1,0:T(8,128)}) %reduce-scatter.2.cloned.1.call-update) | async-done | bytes 14352 | tf_op jit(solution)/shard_map/reduce_scatter | solution.py:56
  453.2 0.0 copy-done.7
  453.2 1.0 convolution_convert_fusion.2
  454.1 0.1 copy.25
  454.3 24.6 %all_to_all.8 = bf16[32,1,4,448]{3,2,1,0:T(4,128)(2,1)S(1)} all-to-all(bf16[32,1,4,448]{3,2,1,0:T(4,128)(2,1)S(1)} %bitcast.62), channel_id=1, replica_groups=mesh['ctx'=32,'grp'=16] {'ctx'}, dimensions={0} | all-to-all | bytes 229376 | tf_op jit(solution)/shard_map/all_to_all | solution.py:89
  478.9 0.0 copy-done
  478.9 1.1 convolution_bitcast_fusion
  480.0 1.1 convolution_bitcast_fusion.1
  481.1 0.0 all-reduce.3.cloned.1.call-update
  481.1 0.0 copy-done.8
  481.1 0.1 reduce_sum.29
  481.2 283.5 %all-reduce.3.cloned.1.call-done = (f32[1,32,4,1024]{3,1,2,0:T(8,128)}, f32[1,32,4,1024]{3,1,2,0:T(8,128)}) async-done(((f32[1,32,4,1024]{3,1,2,0:T(8,128)}, f32[1,32,4,1024]{3,1,2,0:T(8,128)}), (f32[1,32,4,1024]{3,1,2,0:T(8,128)}, f32[1,32,4,1024]{3,1,2,0:T(8,128)})) %all-reduce.3.cloned.1.call-update) | async-done | bytes 1048592 | tf_op jit(solution)/shard_map/psum | solution.py:94
  764.7 1.7 fusion.9
  766.4 0.7 copy.28
  767.1 7.0 all-to-all-start.1
  774.2 0.1 multiply_divide_fusion
  774.2 0.1 mul.53
  774.3 0.3 fusion.27
  774.6 11.6 %all-to-all-done.1 = bf16[1,32,4,448]{3,2,0,1:T(4,128)(2,1)S(1)} async-done(((bf16[1,32,4,448]{3,2,0,1:T(4,128)(2,1)}), bf16[1,32,4,448]{3,2,0,1:T(4,128)(2,1)S(1)}, u32[]{:S(2)}, u32[]{:S(2)}) %all-to-all-start.1) | async-done | bytes 114720 | tf_op jit(solution)/shard_map/all_to_all | solution.py:99
  786.2 0.1 reshape.75
  786.2 0.0 copy-done.6
  786.2 0.8 fusion.13
  (13 shorter events, 0.1 us)
Async XLA Ops:
  6.5 472.3 %copy-start = (bf16[1,448,1024]{2,1,0:T(8,128)(2,1)S(1)}, bf16[1,448,1024]{2,1,0:T(8,128)(2,1)}, u32[]{:S(2)}) copy-start(bf16[1,448,1024]{2,1,0:T(8,128)(2,1)} %param.22) | copy-start | bytes 2752516
  6.5 173.9 %copy-start.5 = (bf16[256,4,64]{0,2,1:T(8,128)(2,1)S(1)}, bf16[256,4,64]{0,2,1:T(8,128)(2,1)}, u32[]{:S(2)}) copy-start(bf16[256,4,64]{0,2,1:T(8,128)(2,1)} %param.13) | copy-start | bytes 393220
  6.5 173.9 %all-gather.2.cloned.1.call-start = ((), (), s32[]{:S(2)}) async-start(), calls=%async_computation.3 | async-start | bytes 7520256 | tf_op jit(solution)/shard_map/all_gather | solution.py:35
  7.3 445.9 %reduce-scatter.2.cloned.1.call-start = ((), (), s32[]{:S(2)}) async-start(), calls=%async_computation.4 | async-start | bytes 540672 | tf_op jit(solution)/shard_map/reduce_scatter | solution.py:56
  180.4 5.1 copy-start.1
  185.5 2.0 copy-start.3
  185.5 37.7 %copy-start.4 = (bf16[512,448]{0,1:T(8,128)(2,1)S(1)}, bf16[512,448]{0,1:T(8,128)(2,1)}, u32[]{:S(2)}) copy-start(bf16[512,448]{0,1:T(8,128)(2,1)} %param.17) | copy-start | bytes 1376260
  187.6 36.9 %copy-start.9 = (s32[8,8]{1,0:T(8,128)S(1)}, s32[8,8]{1,0:T(8,128)}, u32[]{:S(2)}) copy-start(s32[8,8]{1,0:T(8,128)} %param.19) | copy-start | bytes 772
  187.6 265.6 %copy-start.7 = (bf16[8,448]{1,0:T(8,128)(2,1)S(1)}, bf16[8,448]{1,0:T(8,128)(2,1)}, u32[]{:S(2)}) copy-start(bf16[8,448]{1,0:T(8,128)(2,1)} %param.18) | copy-start | bytes 21508
  224.4 255.6 %copy-start.2 = (bf16[1,448,1024]{2,1,0:T(8,128)(2,1)S(1)}, bf16[1,448,1024]{2,1,0:T(8,128)(2,1)}, u32[]{:S(2)}) copy-start(bf16[1,448,1024]{2,1,0:T(8,128)(2,1)} %param.21) | copy-start | bytes 2752516
  224.4 540.3 %all-reduce.3.cloned.1.call-start = ((), (), s32[]{:S(2)}) async-start(), calls=%async_computation.5 | async-start | bytes 2097152 | tf_op jit(solution)/shard_map/psum | solution.py:94
  480.0 1.1 copy-start.8
  480.0 284.7 %copy-start.10 = (bf16[1,1024,448]{1,2,0:T(8,128)(2,1)S(1)}, bf16[1,1024,448]{1,2,0:T(8,128)(2,1)}, u32[]{:S(2)}) copy-start(bf16[1,1024,448]{1,2,0:T(8,128)(2,1)} %param.23) | copy-start | bytes 2752516
  764.7 21.5 %copy-start.6 = (f32[8,448]{1,0:T(8,128)S(1)}, f32[8,448]{1,0:T(8,128)}, u32[]{:S(2)}) copy-start(f32[8,448]{1,0:T(8,128)} %reduce-scatter.2.cloned.1.call-done) | copy-start | bytes 43012
  767.1 19.1 %all-to-all-start.1 = ((bf16[1,32,4,448]{3,2,0,1:T(4,128)(2,1)}), bf16[1,32,4,448]{3,2,0,1:T(4,128)(2,1)S(1)}, u32[]{:S(2)}, u32[]{:S(2)}) async-start(bf16[1,32,4,448]{3,2,0,1:T(4,128)(2,1)} %copy.28), calls=%async_computation.2 | async-start | bytes 262144 | tf_op jit(solution)/shard_map/all_to_all | solution.py:99
Sparse Core Ops, SparseCore 0:
  10.5 169.9 all-gather.1
  224.5 228.5 reduce-scatter.1
  481.2 283.4 all-reduce.2
where the time goes:
time: 794 us
  waiting for transfers between devices  695 us (88%)
  blocking collectives  59.9 us (8%)
  matrix products  15.5 us (2%)
  between operations  13.2 us (2%)
    psum x1, waiting for transfers between devices, per_device(): gate_sum, up_sum = lax.psum((gate_part, up_part), 'grp')  283 us
    reduce_scatter x1, waiting for transfers between devices, per_device(): lax.psum_scatter(jnp.dot(attended, w_out, preferred_element_type=jnp.floa...  228 us
    all_gather x1, waiting for transfers between devices, per_device(): all_keys = lax.all_gather(prompt, 'grp', axis=0, tiled=True)  172 us
    all_gather x1, blocking collectives, per_device(): attended = lax.all_gather(own_rows, 'grp', axis=0, tiled=True)  35.3 us
    all_to_all x1, blocking collectives, per_device(): lax.all_to_all(outgoing, 'ctx', split_axis=0, concat_axis=1, tiled=True)  24.6 us
  transfers between devices with their start and end apart: 4, of which 4 were waited for; matrix products, arithmetic and copies ran while one was open for 0% of the time, Pallas kernels for 0%

commit v1 on v0

--- a/solution.py
+++ b/solution.py
@@ -2,6 +2,7 @@
 import jax.numpy as jnp
 from jax import lax
 from jax.sharding import PartitionSpec as P
+from jax.lax import all_to_all, psum
 
 NOPE = 128
 ROPE = 64
@@ -32,7 +33,10 @@
     queries = jnp.concatenate([q_latent, q_rope], axis=-1)
     head_uv = w_uv.astype(jnp.float32)
     head_cols = queries.shape[1] * VDIM
-    all_keys = lax.all_gather(prompt, "grp", axis=0, tiled=True)
+    begin_ways = lambda local_array, axis_name: jnp.concatenate(
+        all_to_all(jnp.stack(psum(1, axis_name) * [local_array], 0), axis_name, 0, 0), 0
+    )
+    all_keys = begin_ways(prompt, "grp")
     row_share = queries.shape[0] // lax.axis_size("grp")
     own_queries = lax.dynamic_slice_in_dim(queries, lax.axis_index("grp") * row_share, row_share, 0)
     scores = (

time: 794 us -> 1010 us (1.27)
  blocking collectives: 59.9 us -> 179 us
  waiting for transfers between devices: 695 us -> 743 us
  local copies, waits for them, and re-layouts: 1.51 us -> 35.3 us
  starting transfers between devices: 7.12 us -> 25 us
    all_to_all x0 -> x1, waiting for transfers between devices: none -> 179 us  [per_device(): all_to_all(jnp.stack(psum(1, axis_name) * [local_array], 0), axis_name, 0...]
    all_gather x1 -> x0, waiting for transfers between devices: 172 us -> none  [per_device(): all_keys = lax.all_gather(prompt, 'grp', axis=0, tiled=True)]
    all_gather x1, blocking collectives: 35.3 us -> 155 us  [per_device(): attended = lax.all_gather(own_rows, 'grp', axis=0, tiled=True)]
    reduce_scatter x1, waiting for transfers between devices: 228 us -> 268 us  [per_device(): lax.psum_scatter(jnp.dot(attended, w_out, preferred_element_type=jnp.floa...]
    reshape x0 -> x2, local copies, waits for them, and re-layouts: none -> 18.2 us  [per_device(): jnp.concatenate(all_to_all(jnp.stack(psum(1, axis_name) * [local_array],...]
    all_to_all x0 -> x1, starting transfers between devices: none -> 17.8 us  [per_device(): all_to_all(jnp.stack(psum(1, axis_name) * [local_array], 0), axis_name, 0...]
where the time goes in v1:
time: 1010 us
  waiting for transfers between devices  743 us (74%)
  blocking collectives  179 us (18%)
  local copies, waits for them, and re-layouts  35.3 us (3%)
  starting transfers between devices  25 us (2%)
  between operations  13.6 us (1%)
  matrix products  11.7 us (1%)
    psum x1, waiting for transfers between devices, per_device(): gate_sum, up_sum = lax.psum((gate_part, up_part), 'grp')  284 us
    reduce_scatter x1, waiting for transfers between devices, per_device(): lax.psum_scatter(jnp.dot(attended, w_out, preferred_element_type=jnp.floa...  268 us
    all_to_all x1, waiting for transfers between devices, per_device(): all_to_all(jnp.stack(psum(1, axis_name) * [local_array], 0), axis_name, 0...  179 us
    all_gather x1, blocking collectives, per_device(): attended = lax.all_gather(own_rows, 'grp', axis=0, tiled=True)  155 us
    all_to_all x1, blocking collectives, per_device(): lax.all_to_all(outgoing, 'ctx', split_axis=0, concat_axis=1, tiled=True)  24.6 us
  transfers between devices with their start and end apart: 4, of which 4 were waited for; matrix products, arithmetic and copies ran while one was open for 0% of the time, Pallas kernels for 0%

profile of v1, /device:TPU:8, one launch (start us, length us, event | category | flops | bytes accessed | tf_op | source)
XLA Modules:
  0.0 1008.5 jit_solution(18087458745415093508)
XLA Ops:
  6.5 0.0 copy-start
  6.5 4.9 stack.2
  11.5 17.8 %all-to-all-start = ((bf16[16,384,576]{1,2,0:T(8,128)(2,1)}), bf16[16,384,576]{1,2,0:T(8,128)(2,1)}, u32[]{:S(2)}, u32[]{:S(2)}) async-start(bf16[16,384,576]{1,2,0:T(8,128)(2,1)} %stack.2), calls=%async_computation | async-start | bytes 14155776 | tf_op jit(solution)/shard_map/all_to_all | solution.py:37
  29.3 0.0 reduce-scatter.2.cloned.1.call-start
  29.4 0.5 fusion.3
  29.9 178.9 %all-to-all-done = bf16[16,384,576]{1,2,0:T(8,128)(2,1)} async-done(((bf16[16,384,576]{1,2,0:T(8,128)(2,1)}), bf16[16,384,576]{1,2,0:T(8,128)(2,1)}, u32[]{:S(2)}, u32[]{:S(2)}) %all-to-all-start) | async-done | bytes 7077920 | tf_op jit(solution)/shard_map/all_to_all | solution.py:37
  208.8 10.0 copy.22
  218.8 10.9 %reshape.82 = bf16[6144,576,1]{0,1,2:T(8,128)(2,1)} reshape(bf16[16,384,576]{1,0,2:T(8,128)(2,1)} %copy.22) | data formatting | bytes 14155776 | tf_op jit(solution)/shard_map/reshape | solution.py:36
  229.8 7.3 copy.34
  237.0 0.0 copy-done.1
  237.0 1.6 fusion.37
  238.7 0.4 fusion.1
  239.1 1.0 copy-done.2
  240.0 2.0 fusion
  242.1 0.0 copy-done.5
  242.1 0.0 copy-start.12
  242.1 0.0 copy-start.10
  242.1 0.3 fusion.7
  242.5 154.7 %all_gather.3 = bf16[256,512]{1,0:T(8,128)(2,1)S(1)} all-gather(bf16[16,512]{1,0:T(8,128)(2,1)S(1)} %bitcast.62), channel_id=1, replica_groups=mesh['ctx'=32,'grp'=16] {'grp'}, dimensions={0}, use_global_device_ids=true | all-gather | bytes 278528 | tf_op jit(solution)/shard_map/all_gather | solution.py:58
  397.2 1.1 fusion.38
  398.3 0.0 reduce-scatter.2.cloned.1.call-update
  398.3 0.0 all-reduce.3.cloned.1.call-start
  398.4 0.0 copy-done.12
  398.4 0.1 reshape.74
  398.4 0.1 fusion.24
  398.5 0.1 reduce_window_sum.11
  398.6 0.2 select_reduce_fusion
  398.8 0.3 convolution_convert_fusion.3
  399.1 268.4 %reduce-scatter.2.cloned.1.call-done = f32[8,448]{1,0:T(8,128)} async-done(((f32[256,448]{1,0:T(8,128)}), f32[8,448]{1,0:T(8,128)}) %reduce-scatter.2.cloned.1.call-update) | async-done | bytes 14352 | tf_op jit(solution)/shard_map/reduce_scatter | solution.py:60
  667.4 0.0 copy-done.10
  667.4 1.0 convolution_convert_fusion.2
  668.4 0.1 copy.26
  668.6 24.6 %all_to_all.23 = bf16[32,1,4,448]{3,2,1,0:T(4,128)(2,1)S(1)} all-to-all(bf16[32,1,4,448]{3,2,1,0:T(4,128)(2,1)S(1)} %bitcast.61), channel_id=1, replica_groups=mesh['ctx'=32,'grp'=16] {'ctx'}, dimensions={0} | all-to-all | bytes 229376 | tf_op jit(solution)/shard_map/all_to_all | solution.py:93
  693.2 1.1 convolution_bitcast_fusion
  694.3 0.0 copy-done.3
  694.3 1.1 convolution_bitcast_fusion.1
  695.4 0.0 all-reduce.3.cloned.1.call-update
  695.4 0.1 reduce_sum.29
  695.5 283.8 %all-reduce.3.cloned.1.call-done = (f32[1,32,4,1024]{3,1,2,0:T(8,128)}, f32[1,32,4,1024]{3,1,2,0:T(8,128)}) async-done(((f32[1,32,4,1024]{3,1,2,0:T(8,128)}, f32[1,32,4,1024]{3,1,2,0:T(8,128)}), (f32[1,32,4,1024]{3,1,2,0:T(8,128)}, f32[1,32,4,1024]{3,1,2,0:T(8,128)})) %all-reduce.3.cloned.1.call-update) | async-done | bytes 1048592 | tf_op jit(solution)/shard_map/psum | solution.py:98
  979.3 1.7 fusion.4
  981.0 0.8 copy.29
  981.7 7.0 all-to-all-start.2
  988.8 0.1 multiply_divide_fusion
  988.9 0.1 mul.53
  988.9 0.3 fusion.22
  989.2 11.6 %all-to-all-done.2 = bf16[1,32,4,448]{3,2,0,1:T(4,128)(2,1)S(1)} async-done(((bf16[1,32,4,448]{3,2,0,1:T(4,128)(2,1)}), bf16[1,32,4,448]{3,2,0,1:T(4,128)(2,1)S(1)}, u32[]{:S(2)}, u32[]{:S(2)}) %all-to-all-start.2) | async-done | bytes 114720 | tf_op jit(solution)/shard_map/all_to_all | solution.py:103
  1000.8 0.1 reshape.81
  1000.9 0.8 fusion.8
  (22 shorter events, 0.1 us)
Async XLA Ops:
  6.5 686.6 %copy-start = (bf16[1,448,1024]{2,1,0:T(8,128)(2,1)S(1)}, bf16[1,448,1024]{2,1,0:T(8,128)(2,1)}, u32[]{:S(2)}) copy-start(bf16[1,448,1024]{2,1,0:T(8,128)(2,1)} %param.22) | copy-start | bytes 2752516
  11.5 17.9 %copy-start.4 = (bf16[4,128,512]{2,1,0:T(8,128)(2,1)S(1)}, bf16[4,128,512]{2,1,0:T(8,128)(2,1)}, u32[]{:S(2)}) copy-start(bf16[4,128,512]{2,1,0:T(8,128)(2,1)} %param.14) | copy-start | bytes 1572868
  11.5 17.9 %copy-start.7 = (bf16[256,4,128]{2,1,0:T(4,128)(2,1)S(1)}, bf16[256,4,128]{2,1,0:T(4,128)(2,1)}, u32[]{:S(2)}) copy-start(bf16[256,4,128]{2,1,0:T(4,128)(2,1)} %param.12) | copy-start | bytes 786436
  11.5 197.4 %all-to-all-start = ((bf16[16,384,576]{1,2,0:T(8,128)(2,1)}), bf16[16,384,576]{1,2,0:T(8,128)(2,1)}, u32[]{:S(2)}, u32[]{:S(2)}) async-start(bf16[16,384,576]{1,2,0:T(8,128)(2,1)} %stack.2), calls=%async_computation | async-start | bytes 14155776 | tf_op jit(solution)/shard_map/all_to_all | solution.py:37
  29.3 638.1 %reduce-scatter.2.cloned.1.call-start = ((), (), s32[]{:S(2)}) async-start(), calls=%async_computation.4 | async-start | bytes 540672 | tf_op jit(solution)/shard_map/reduce_scatter | solution.py:60
  229.8 7.3 copy-start.1
  229.8 7.3 copy-start.8
  237.0 3.0 copy-start.2
  240.0 2.0 copy-start.5
  240.0 157.1 %copy-start.6 = (bf16[512,448]{0,1:T(8,128)(2,1)S(1)}, bf16[512,448]{0,1:T(8,128)(2,1)}, u32[]{:S(2)}) copy-start(bf16[512,448]{0,1:T(8,128)(2,1)} %param.17) | copy-start | bytes 1376260
  242.1 156.3 %copy-start.12 = (s32[8,8]{1,0:T(8,128)S(1)}, s32[8,8]{1,0:T(8,128)}, u32[]{:S(2)}) copy-start(s32[8,8]{1,0:T(8,128)} %param.19) | copy-start | bytes 772
  242.1 425.3 %copy-start.10 = (bf16[8,448]{1,0:T(8,128)(2,1)S(1)}, bf16[8,448]{1,0:T(8,128)(2,1)}, u32[]{:S(2)}) copy-start(bf16[8,448]{1,0:T(8,128)(2,1)} %param.18) | copy-start | bytes 21508
  398.3 296.0 %copy-start.3 = (bf16[1,448,1024]{2,1,0:T(8,128)(2,1)S(1)}, bf16[1,448,1024]{2,1,0:T(8,128)(2,1)}, u32[]{:S(2)}) copy-start(bf16[1,448,1024]{2,1,0:T(8,128)(2,1)} %param.21) | copy-start | bytes 2752516
  398.3 581.0 %all-reduce.3.cloned.1.call-start = ((), (), s32[]{:S(2)}) async-start(), calls=%async_computation.5 | async-start | bytes 2097152 | tf_op jit(solution)/shard_map/psum | solution.py:98
  694.3 1.1 copy-start.11
  694.3 285.0 %copy-start.13 = (bf16[1,1024,448]{1,2,0:T(8,128)(2,1)S(1)}, bf16[1,1024,448]{1,2,0:T(8,128)(2,1)}, u32[]{:S(2)}) copy-start(bf16[1,1024,448]{1,2,0:T(8,128)(2,1)} %param.23) | copy-start | bytes 2752516
  979.3 21.5 %copy-start.9 = (f32[8,448]{1,0:T(8,128)S(1)}, f32[8,448]{1,0:T(8,128)}, u32[]{:S(2)}) copy-start(f32[8,448]{1,0:T(8,128)} %reduce-scatter.2.cloned.1.call-done) | copy-start | bytes 43012
  981.7 19.1 %all-to-all-start.2 = ((bf16[1,32,4,448]{3,2,0,1:T(4,128)(2,1)}), bf16[1,32,4,448]{3,2,0,1:T(4,128)(2,1)S(1)}, u32[]{:S(2)}, u32[]{:S(2)}) async-start(bf16[1,32,4,448]{3,2,0,1:T(4,128)(2,1)} %copy.29), calls=%async_computation.3 | async-start | bytes 262144 | tf_op jit(solution)/shard_map/all_to_all | solution.py:103
Sparse Core Ops, SparseCore 0:
  398.4 268.9 reduce-scatter.1
  695.5 283.7 all-reduce.2
